TPU v7x, 512 devices: a whole 4x4x16 slice. The times are simulated.
512 devices in a mesh: dp: 4 (over y), emb: 128 (over x, z, core).
Axes of the slice: x: 4, y: 4, z: 16, core: 2. Of those that a mesh axis runs over, the one named last changes fastest.
Arguments:
- history: bfloat16 [512, 256, 512], P(('dp', 'emb')), may hold values from -6 to 6
- dout: bfloat16 [512, 256, 512], P(('dp', 'emb')), may hold values from -6 to 6
- lengths: int32 [512], P(('dp', 'emb')), may hold values from 1 to 256, 65536 in all
- item_ids: int32 [512, 256], P(('dp', 'emb')), may hold values from 0 to 32767, as said below
- row_place: int32 [32768], replicated, may hold values from 0 to 32767, as said below
- w1: bfloat16 [2048, 512], replicated, may hold values from -0.25 to 0.25
Outputs:
- table_grad: float32 [32768, 512], P('emb')
- weight_grad: float32 [2048, 512], P(('dp', 'emb'))
Inputs may be any that keep to these rules, and one draw needn't show every extreme that they name: `row_place`: A permutation of the table rows. `item_ids`: among the positions of one device's users, at most 4 name rows placed on any one shard; in every draw some shard gets exactly 4 from every device.
All inputs are finite; a program needn't handle non-finite values. No bound on the sum of `lengths` on one device may be relied on, other than what follows from the above.
Results may differ from a plain program's by a relative error of at most 0.0085.
Values may be sent and summed in bfloat16 or wider, within the bound.
A program may use at most 64 MiB of HBM per device.

v0:
```python
import jax
import jax.numpy as jnp
from jax import lax
from jax.sharding import PartitionSpec as P

HEAD = 64


eps = 1e-05


def layer_norm(value):
    centred = value - jnp.mean(value, axis=-1, keepdims=True)
    rstd = lax.rsqrt(jnp.mean(centred * centred, axis=-1, keepdims=True) + eps)
    return (centred * rstd, rstd)


def norm_back(grad, normed, rstd):
    return rstd * (
        grad
        - jnp.mean(grad, axis=-1, keepdims=True)
        - normed * jnp.mean(grad * normed, axis=-1, keepdims=True)
    )


def user_grads(hist, cot, w1, length):
    seq = hist.shape[0]
    width = hist.shape[1]
    head = HEAD
    heads = width // head
    scale = 1.0 / head**0.5
    positions = jnp.arange(seq, dtype=jnp.int32)
    valid = positions < length
    inverse_len = 1.0 / length.astype(jnp.float32)
    xfull = hist.astype(jnp.float32)
    xnorm, rstd_x = layer_norm(xfull)
    xn = xnorm.astype(jnp.bfloat16)
    gates = lax.dot_general(xn, w1, (((1,), (1,)), ((), ())), preferred_element_type=jnp.float32)
    sig_g = jax.nn.sigmoid(gates)
    act = (gates * sig_g).astype(jnp.bfloat16)
    u_act = act[:, :width]
    v_act = act[:, width : 2 * width].reshape(seq, heads, head)
    q_act = act[:, 2 * width : 3 * width].reshape(seq, heads, head)
    k_act = act[:, 3 * width :].reshape(seq, heads, head)
    mask = ((positions[None, :] <= positions[:, None]) & valid[:, None] & valid[None, :]).astype(
        jnp.float32
    )
    scores = jnp.einsum("ihe,jhe->hij", q_act, k_act, preferred_element_type=jnp.float32) * scale
    sig_s = jax.nn.sigmoid(scores)
    probs = (scores * sig_s * mask * inverse_len).astype(jnp.bfloat16)
    attended = jnp.einsum("hij,jhe->ihe", probs, v_act, preferred_element_type=jnp.float32).reshape(
        seq, width
    )
    o_norm, rstd_o = layer_norm(attended)
    dy = cot.astype(jnp.float32) * valid[:, None].astype(jnp.float32)
    d_u = dy * o_norm
    d_on = dy * u_act.astype(jnp.float32)
    d_o = norm_back(d_on, o_norm, rstd_o).astype(jnp.bfloat16).reshape(seq, heads, head)
    d_p = jnp.einsum("ihe,jhe->hij", d_o, v_act, preferred_element_type=jnp.float32)
    d_v = jnp.einsum("hij,ihe->jhe", probs, d_o, preferred_element_type=jnp.float32)
    d_s = (d_p * (sig_s * (1.0 + scores * (1.0 - sig_s))) * mask * (inverse_len * scale)).astype(
        jnp.bfloat16
    )
    d_q = jnp.einsum("hij,jhe->ihe", d_s, k_act, preferred_element_type=jnp.float32)
    d_k = jnp.einsum("hij,ihe->jhe", d_s, q_act, preferred_element_type=jnp.float32)
    d_act = jnp.concatenate(
        [d_u, d_v.reshape(seq, width), d_q.reshape(seq, width), d_k.reshape(seq, width)], axis=1
    )
    d_g = (d_act * (sig_g * (1.0 + gates * (1.0 - sig_g)))).astype(jnp.bfloat16)
    d_xn = jnp.dot(d_g, w1, preferred_element_type=jnp.float32)
    d_x = norm_back(d_xn, xnorm, rstd_x) + dy
    d_x = jnp.where(valid[:, None], d_x, 0.0).astype(jnp.bfloat16)
    return (d_x, d_g, xn)


def shard_sum(places, rows_dev, rows):
    flat_rows = rows.reshape(-1, rows.shape[-1])
    onehot = (places.reshape(-1)[:, None] == jnp.arange(rows_dev, dtype=jnp.int32)[None, :]).astype(
        jnp.bfloat16
    )
    return lax.dot_general(
        onehot, flat_rows, (((0,), (0,)), ((), ())), preferred_element_type=jnp.float32
    )


def body(history, dout, lengths, item_ids, row_place, w1):
    width = history.shape[2]
    d_x, d_g, xn = user_grads(history[0], dout[0], w1, lengths[0])
    grads_x = d_x
    grads_g = d_g
    normals = xn
    d_x = grads_x
    d_g = grads_g
    xn = normals
    weight_grad = lax.psum_scatter(
        lax.dot_general(d_g, xn, (((0,), (0,)), ((), ())), preferred_element_type=jnp.float32),
        ("dp", "emb"),
        scatter_dimension=0,
        tiled=True,
    )
    group = lax.axis_size("emb")
    tokens = d_x.shape[0]
    capacity = 2 * tokens // group
    rows_dev = row_place.shape[0] // group
    places = row_place[item_ids.reshape(-1)]
    owner = places // rows_dev
    local_row = places % rows_dev
    owner_hits = (owner[:, None] == jnp.arange(group, dtype=jnp.int32)[None, :]).astype(jnp.int32)
    rank = jnp.sum(jnp.cumsum(owner_hits, axis=0) * owner_hits, axis=1) - 1
    slot = owner * capacity + rank
    outgoing = (
        jnp.zeros((group * capacity, width), jnp.bfloat16)
        .at[slot]
        .set(d_x)
        .reshape(group, capacity, width)
    )
    targets = (
        jnp.full((group * capacity,), rows_dev, jnp.int32)
        .at[slot]
        .set(local_row)
        .reshape(group, capacity)
    )
    every_target = lax.all_gather(targets, "dp", axis=1, tiled=True)
    every_row = lax.all_gather(outgoing, "dp", axis=1, tiled=True)
    arrived = lax.all_to_all(every_target, "emb", split_axis=0, concat_axis=0, tiled=True)
    table_grad = shard_sum(
        arrived, rows_dev, lax.all_to_all(every_row, "emb", split_axis=0, concat_axis=0, tiled=True)
    )
    return (table_grad, weight_grad)


def solution(mesh):
    return jax.shard_map(
        body,
        mesh=mesh,
        in_specs=(
            P(("dp", "emb"), None, None),
            P(("dp", "emb"), None, None),
            P(("dp", "emb")),
            P(("dp", "emb"), None),
            P(),
            P(),
        ),
        out_specs=(P("emb", None), P(("dp", "emb"), None)),
        check_vma=False,
    )
```

profile of v0, /device:TPU:1, one launch (start us, length us, event | category | flops | bytes accessed | tf_op | source)
XLA Modules:
  0.0 654.4 jit_solution(2540504110276902588)
XLA Ops:
  8.0 0.0 copy-start
  8.0 0.0 all-gather.3.cloned.1.call-start
  8.1 1.2 convert_reduce_fusion
  9.3 1.2 fusion.15
  10.5 3.1 multiply_convert_fusion.2
  13.5 1.0 copy-done.5
  14.5 0.1 fusion.47
  14.6 0.1 copy.49
  14.7 0.1 copy.50
  15.5 0.1 fusion.34
  15.7 0.1 copy.48
  15.9 2.1 multiply_convert_fusion.1
  18.0 0.0 copy-start.4
  18.0 0.5 fusion.48
  18.5 0.1 fusion.19
  18.6 0.4 copy-done.2
  19.0 0.2 copy.51
  19.2 2.0 fusion.20
  21.2 1.2 multiply_convert_fusion.3
  22.4 0.1 copy.52
  22.6 1.5 fusion.49
  24.1 2.8 multiply_convert_fusion
  26.9 0.0 copy-start.14
  27.0 0.0 copy-start.1
  27.0 0.4 fusion.50
  27.4 1.1 fusion.51
  28.5 1.7 gather_fusion
  30.3 0.6 and_select_fusion.1
  30.9 1.0 copy.53
  31.9 1.0 copy.54
  32.9 2.1 copy.55
  34.9 3.0 fusion
  37.9 1.5 fusion.46
  39.5 0.6 broadcast_multiply_fusion
  40.1 0.5 broadcast_multiply_fusion.1
  40.6 0.7 copy.44
  41.3 1.0 fusion.35
  42.4 0.6 slice_bitcast_fusion
  43.0 1.3 reduce-window.9
  44.2 0.7 slice.19
  45.0 0.8 fusion.36
  45.8 3.1 scatter_custom_fusion.1
  48.9 2.0 reshape.276
  50.9 1.9 copy.56
  52.8 0.0 all-gather.3.cloned.1.call-update
  52.8 1.6 scatter_custom_fusion
  54.4 0.1 reshape.267
  54.5 0.1 copy.46
  54.6 9.4 %all-gather = s32[4,4,128]{2,1,0:T(4,128)S(1)} all-gather(s32[1,4,128]{2,1,0:T(4,128)S(1)} %copy.46), channel_id=1, replica_groups=mesh['dp'=4,'emb'=128] {'dp'}, dimensions={0}, use_global_device_ids=true | all-gather | bytes 10240 | tf_op jit(solution)/shard_map/all_gather | solution.py:123
  64.0 0.7 copy.47
  64.8 22.2 %all-to-all-start = ((s32[128,1,16]{2,1,0:T(1,128)}), s32[128,1,16]{2,1,0:T(1,128)S(1)}, u32[]{:S(2)}, u32[]{:S(2)}) async-start(s32[128,1,16]{2,1,0:T(1,128)} %copy.47), calls=%async_computation | async-start | bytes 131072 | tf_op jit(solution)/shard_map/all_to_all | solution.py:125
  87.0 9.9 %all-gather.3.cloned.1.call-done = bf16[128,16,512]{2,0,1:T(8,128)(2,1)} async-done(((bf16[128,4,512]{2,0,1:T(8,128)(2,1)}), bf16[128,16,512]{2,0,1:T(8,128)(2,1)}) %all-gather.3.cloned.1.call-update) | async-done | bytes 2097168 | tf_op jit(solution)/shard_map/all_gather | solution.py:124
  96.8 4.1 copy.57
  101.0 0.9 all-to-all-done
  101.9 16.1 %all-to-all-start.1 = ((bf16[128,16,512]{2,1,0:T(8,128)(2,1)}), bf16[128,16,512]{2,1,0:T(8,128)(2,1)}, u32[]{:S(2)}, u32[]{:S(2)}) async-start(bf16[128,16,512]{2,1,0:T(8,128)(2,1)} %copy.57), calls=%async_computation.1 | async-start | bytes 4194304 | tf_op jit(solution)/shard_map/all_to_all | solution.py:127
  118.1 0.0 all-reduce.3.cloned.1.call-start
  118.1 2.8 fusion.42
  120.9 0.0 all-reduce.3.cloned.1.call-update
  120.9 0.5 broadcast.325
  121.5 0.8 reduce.7
  122.3 0.1 eq.44
  122.4 519.8 %all-reduce.3.cloned.1.call-done = f32[2048,512]{1,0:T(8,128)} async-done(((f32[2048,512]{1,0:T(8,128)}), f32[2048,512]{1,0:T(8,128)}) %all-reduce.3.cloned.1.call-update) | async-done | bytes 4194320
  642.2 1.3 constant_dynamic-slice_fusion
  643.5 3.5 fusion.1
  (40 shorter events, 0.2 us)
Async XLA Ops:
  8.0 2.5 copy-start
  8.0 88.8 %all-gather.3.cloned.1.call-start = ((), (), s32[]{:S(2)}) async-start(), calls=%async_computation.2 | async-start | bytes 2621440 | tf_op jit(solution)/shard_map/all_gather | solution.py:124
  13.5 1.0 copy-start.5
  14.7 1.1 copy-start.6
  14.9 3.1 copy-start.8
  15.5 2.4 copy-start.13
  15.6 2.3 copy-start.12
  15.8 2.2 copy-start.10
  18.0 1.0 copy-start.2
  18.0 1.2 copy-start.4
  21.2 2.9 copy-start.11
  24.1 2.8 copy-start.9
  24.1 3.3 copy-start.7
  26.9 1.6 copy-start.14
  27.0 1.6 copy-start.1
  34.9 3.0 copy-start.3
  64.8 37.2 %all-to-all-start = ((s32[128,1,16]{2,1,0:T(1,128)}), s32[128,1,16]{2,1,0:T(1,128)S(1)}, u32[]{:S(2)}, u32[]{:S(2)}) async-start(s32[128,1,16]{2,1,0:T(1,128)} %copy.47), calls=%async_computation | async-start | bytes 131072 | tf_op jit(solution)/shard_map/all_to_all | solution.py:125
  101.9 541.6 %all-to-all-start.1 = ((bf16[128,16,512]{2,1,0:T(8,128)(2,1)}), bf16[128,16,512]{2,1,0:T(8,128)(2,1)}, u32[]{:S(2)}, u32[]{:S(2)}) async-start(bf16[128,16,512]{2,1,0:T(8,128)(2,1)} %copy.57), calls=%async_computation.1 | async-start | bytes 4194304 | tf_op jit(solution)/shard_map/all_to_all | solution.py:127
  118.1 524.1 %all-reduce.3.cloned.1.call-start = ((), (), s32[]{:S(2)}) async-start(), calls=%async_computation.3 | async-start | bytes 8388608
Sparse Core Ops, SparseCore 0:
  53.0 43.8 all-gather.2
Sparse Core Ops, SparseCore 1:
  124.0 518.1 all-reduce.2
where the time goes:
time: 657 us; the launch traced here: 654 us
  waiting for transfers between devices  531 us (81%)
  starting transfers between devices  38.4 us (6%)
  local copies, waits for them, and re-layouts  22.4 us (3%)
  matrix products  19.2 us (3%)
  other arithmetic  17.7 us (3%)
  between operations  16.6 us (3%)
  blocking collectives  9.45 us (1%)
    unnamed x3, waiting for transfers between devices  520 us
    all_to_all x1, starting transfers between devices, body(): lax.all_to_all(every_target, 'emb', split_axis=0, concat_axis=0, tiled=True)  22.2 us
    all_to_all x1, starting transfers between devices, body(): lax.all_to_all(every_row, 'emb', split_axis=0, concat_axis=0, tiled=True)  16.1 us
  transfers between devices with their start and end apart: 4, of which 3 were waited for; matrix products, arithmetic and copies ran while one was open for 2% of the time, Pallas kernels for 0%

commit v1 on v0

v1 whole, which is shorter than its diff:
```python
import functools

import jax
import jax.numpy as jnp
from jax import lax
from jax.experimental import pallas as pl
from jax.experimental.pallas import tpu as pltpu
from jax.sharding import PartitionSpec as P

MESH = pl.DeviceIdType.MESH
F32 = jnp.float32
BF16 = jnp.bfloat16
EPS = 1e-05

SEQ = 256
D = 512
HEADS = 8
CAP = 4
NY, NX, NZ, NC = 4, 4, 16, 2

LANES = tuple((xs, cs) for xs in (0, 1, 3, 2) for cs in (0, 1))
GROUPS = ((0, 1), (1, 2), (2, 4), (4, 6), (6, 8))
STEPS_Z = tuple(sorted(range(1, NZ), key=lambda d: -min(d, NZ - d)))
STEPS_4 = (2, 1, 3)


def iota(shape, dim):
    return lax.broadcasted_iota(jnp.int32, shape, dim)


def dot_nn(a, b):
    return lax.dot_general(a, b, (((1,), (0,)), ((), ())), preferred_element_type=F32)


def dot_nt(a, b):
    return lax.dot_general(a, b, (((1,), (1,)), ((), ())), preferred_element_type=F32)


def dot_tn(a, b):
    return lax.dot_general(a, b, (((0,), (0,)), ((), ())), preferred_element_type=F32)


def silu_and_slope(value):
    sig = 0.5 * jnp.tanh(0.5 * value) + 0.5
    act = value * sig
    return act, sig + act * (1.0 - sig)


def layer_norm(value):
    centred = value - jnp.mean(value, axis=-1, keepdims=True)
    rstd = lax.rsqrt(jnp.mean(centred * centred, axis=-1, keepdims=True) + EPS)
    return centred * rstd, rstd


def norm_back(grad, normed, rstd):
    return rstd * (
        grad
        - jnp.mean(grad, axis=-1, keepdims=True)
        - normed * jnp.mean(grad * normed, axis=-1, keepdims=True)
    )


class Sems:
    def __init__(self, send, recv):
        self.send, self.recv, self.used = send, recv, 0

    def copy(self, src, dst, device):
        at = self.used
        self.used += 1
        made = pltpu.make_async_remote_copy(
            src_ref=src,
            dst_ref=dst,
            send_sem=self.send.at[at],
            recv_sem=self.recv.at[at],
            device_id=device,
            device_id_type=MESH,
        )
        made.start()
        return made


N_COPIES = 7 + 15 + 7 + 15 * len(GROUPS) + 1 + 6 + 6 + 15 + 1 + 3 + 3


def kernel(
    hist_ref, dout_ref, len_ref, ids_ref, place_ref, w1_ref,
    table_ref, weight_ref,
    xnorm, xn, act, slope, probs, sslope, attn, d_o, d_g,
    slot_s, meta_s, meta_1, meta_z, meta_2, where_s,
    out_s, lane_s, far_s, total_s, ty_s, ty_r, tg_s, tg_r,
    dw_own, dw_s, dw_r, xa_s, xa_r, xb_s, xb_r, a_own, b_own, ya_s, ya_r, yb_s, yb_r,
    zt_own, zt_s, zt_r, fin_s, fin_r,
    send, recv,
):
    y = lax.axis_index("dp")
    emb = lax.axis_index("emb")
    x = emb // (NZ * NC)
    z = lax.rem(emb // NC, NZ)
    c = lax.rem(emb, NC)

    def place(dy, dx, dz, dc):
        return (
            lax.rem(y + dy, NY),
            (lax.rem(x + dx, NX) * NZ + lax.rem(z + dz, NZ)) * NC + lax.rem(c + dc, NC),
        )

    partners = [place(0, xs, 0, cs) for xs, cs in LANES[1:]]
    partners += [place(0, 0, d, 0) for d in STEPS_Z]
    partners += [place(d, 0, 0, 0) for d in STEPS_4]
    barrier = pltpu.get_barrier_semaphore()
    for partner in partners:
        pl.semaphore_signal(barrier, inc=1, device_id=partner, device_id_type=MESH)

    sems = Sems(send, recv)
    started = []

    def remote(src, dst, device):
        made = sems.copy(src, dst, device)
        started.append(made)
        return made

    rows_i, cols_i = iota((SEQ, SEQ), 0), iota((SEQ, SEQ), 1)
    eye = rows_i == cols_i
    ids_row = ids_ref[...].astype(F32)
    ids = jnp.sum(jnp.where(eye, ids_row, 0.0), axis=1, keepdims=True).astype(jnp.int32)
    high = (cols_i == ids // 128).astype(BF16)
    lane128 = iota((SEQ, 128), 1)
    low = lane128 == lax.rem(ids, 128)
    places = place_ref[...]
    owners = dot_nn(high, (places // 256).astype(BF16))
    owner = jnp.sum(jnp.where(low, owners, 0.0), axis=1, keepdims=True).astype(jnp.int32)
    locals_ = dot_nn(high, lax.rem(places, 256).astype(BF16))
    local = jnp.sum(jnp.where(low, locals_, 0.0), axis=1, keepdims=True)
    step_x = lax.rem(owner // 32 - x + NX, NX)
    step_z = lax.rem(lax.rem(owner // 2, 16) - z + NZ, NZ)
    step_c = lax.rem(lax.rem(owner, 2) - c + NC, NC)
    order_x = jnp.where(step_x == 2, 3, jnp.where(step_x == 3, 2, step_x))
    block = ((order_x * NC + step_c) * NZ + step_z).astype(F32)
    block_row = jnp.sum(jnp.where(eye, block, 0.0), axis=0, keepdims=True)
    before = (block == block_row) & (cols_i < rows_i)
    rank = jnp.sum(jnp.where(before, 1.0, 0.0), axis=1, keepdims=True)
    slot = block * CAP + rank
    slot_s[...] = jnp.broadcast_to(jnp.sum(jnp.where(eye, slot, 0.0), axis=0, keepdims=True), (8, SEQ))
    for lane in range(8):
        wanted = (lane128 + lane * NZ * CAP).astype(F32)
        hit = (slot == wanted) & (lane128 < NZ * CAP)
        found = jnp.sum(jnp.where(hit, local - 256.0, 0.0), axis=0, keepdims=True) + 256.0
        meta = jnp.broadcast_to(found, (8, 128))
        if lane:
            meta_s[lane] = meta
        else:
            meta_1[0] = meta

    length = len_ref[...]
    inverse_len = 1.0 / length.astype(F32)
    valid = iota((SEQ, 1), 0) < length
    normed, rstd_x = layer_norm(hist_ref[0].astype(F32))
    xnorm[...] = normed
    xn[...] = normed.astype(BF16)
    for at in range(0, 4 * D, 256):
        gate = dot_nt(xn[...], w1_ref[at : at + 256, :])
        value, slant = silu_and_slope(gate)
        act[:, at : at + 256] = value.astype(BF16)
        slope[:, at : at + 256] = slant

    scale = 1.0 / 64**0.5
    mask = jnp.where((cols_i <= rows_i) & valid & (cols_i < length), inverse_len, 0.0)
    first = iota((SEQ, 128), 1) < 64
    zero = jnp.zeros((SEQ, 128), BF16)

    def split(value):
        return jnp.where(first, value, zero), jnp.where(first, zero, value)

    for pair in range(HEADS // 2):
        at = pair * 128
        v = act[:, D + at : D + at + 128]
        k = act[:, 3 * D + at : 3 * D + at + 128]
        total = None
        for half, (q, v_half) in enumerate(
            zip(split(act[:, 2 * D + at : 2 * D + at + 128]), split(v), strict=True)
        ):
            value, slant = silu_and_slope(dot_nt(q, k) * scale)
            prob = (value * mask).astype(BF16)
            probs[2 * pair + half] = prob
            sslope[2 * pair + half] = slant * (mask * scale)
            term = dot_nn(prob, v_half)
            total = term if total is None else total + term
        attn[:, at : at + 128] = total

    pl.semaphore_wait(barrier, len(partners))
    meta_copies = {
        lane: remote(meta_s.at[lane], meta_1.at[lane], place(0, xs, 0, cs))
        for lane, (xs, cs) in enumerate(LANES)
        if lane
    }

    o_norm, rstd_o = layer_norm(attn[...])
    dy = jnp.where(valid, dout_ref[0].astype(F32), 0.0)
    d_g[:, :D] = (dy * o_norm * slope[:, :D]).astype(BF16)
    d_on = dy * act[:, :D].astype(F32)
    d_o[...] = norm_back(d_on, o_norm, rstd_o).astype(BF16)

    meta_z_copies = []
    for pair in range(HEADS // 2):
        at = pair * 128
        v = act[:, D + at : D + at + 128]
        qs = split(act[:, 2 * D + at : 2 * D + at + 128])
        ks = split(act[:, 3 * D + at : 3 * D + at + 128])
        dos = split(d_o[:, at : at + 128])
        d_v = d_q = d_k = None
        for half in range(2):
            d_p = dot_nt(dos[half], v)
            d_s = (d_p * sslope[2 * pair + half]).astype(BF16)
            terms = (
                dot_tn(probs[2 * pair + half], dos[half]),
                dot_nn(d_s, ks[half]),
                dot_tn(d_s, qs[half]),
            )
            if half:
                d_v, d_q, d_k = d_v + terms[0], d_q + terms[1], d_k + terms[2]
            else:
                d_v, d_q, d_k = terms
        for part, grad in enumerate((d_v, d_q, d_k), 1):
            cols = slice(part * D + at, part * D + at + 128)
            d_g[:, cols] = (grad * slope[:, cols]).astype(BF16)
        if pair == 2:
            tile_row = iota((8, 128), 0)
            gathered = jnp.where(tile_row == 0, meta_1[0], 0.0)
            for lane, copy in meta_copies.items():
                copy.wait_recv()
                gathered += jnp.where(tile_row == lane, meta_1[lane], 0.0)
            meta_z[...] = gathered
            meta_z_copies = [remote(meta_z, meta_2.at[d], place(0, 0, d, 0)) for d in STEPS_Z]

    d_xn = dot_nn(d_g[...], w1_ref[...])
    d_x = norm_back(d_xn, xnorm[...], rstd_x) + dy
    d_x = jnp.where(valid, d_x, 0.0).astype(BF16)

    def pack(lane):
        line = iota((SEQ, SEQ), 0)
        wanted = (line // 16) * CAP + lax.rem(line, CAP) + lane * NZ * CAP
        pick = (wanted.astype(F32) == slot_s[0:1, :]).astype(BF16)
        moved = dot_nn(pick, d_x)
        quarter = lax.rem(iota((SEQ, 128), 0), 16) // CAP
        rows = moved[:, 0:128]
        for j in range(1, 4):
            rows = jnp.where(quarter == j, moved[:, 128 * j : 128 * j + 128], rows)
        return rows.astype(BF16).reshape(NZ, 16, 128)

    far_copies = [None] * len(GROUPS)

    def pass_on(group):
        low_lane, high_lane = GROUPS[group]
        far_copies[group] = [
            remote(
                lane_s.at[pl.ds(low_lane, high_lane - low_lane), d],
                far_s.at[pl.ds(low_lane, high_lane - low_lane), d],
                place(0, 0, d, 0),
            )
            for d in STEPS_Z
        ]

    lane_copies = {}
    lane_s[0] = pack(0)
    pass_on(0)
    for lane in (1, 6, 7, 2, 3, 4, 5):
        xs, cs = LANES[lane]
        out_s[lane] = pack(lane)
        lane_copies[lane] = remote(out_s.at[lane], lane_s.at[lane], place(0, xs, 0, cs))

    is_first = c == 0
    for block_at in range(8):
        share = dot_tn(d_g[:, 256 * block_at : 256 * block_at + 256], xn[...])
        left, right = share[:, :256], share[:, 256:]
        own = jnp.where(is_first, left, right)
        other = jnp.where(is_first, right, left).astype(BF16)
        for part in range(2):
            for sub in range(2):
                cut = (slice(128 * sub, 128 * sub + 128), slice(128 * part, 128 * part + 128))
                to = 2 * block_at + sub
                dw_own[part, to // 4, to % 4] = own[cut]
                dw_s[part, to // 4, to % 4] = other[cut]
    dw_copy = remote(dw_s, dw_r, place(0, 0, 0, 1))

    lane_copies[1].wait_recv()
    pass_on(1)
    for group in (2, 3, 4):
        for lane in range(*GROUPS[group]):
            lane_copies[lane].wait_recv()
        pass_on(group)

    dw_copy.wait_recv()
    for i in range(4):
        dw_own[0, i] += dw_r[0, i].astype(F32)
        xa_s[i] = dw_own[0, i].astype(BF16)
        dw_own[1, i] += dw_r[1, i].astype(F32)
        xb_s[i] = dw_own[1, i].astype(BF16)
    xa_copies = [remote(xa_s.at[:, lax.rem(x + d, NX)], xa_r.at[d - 1], place(0, d, 0, 0)) for d in STEPS_4]
    xb_copies = [remote(xb_s.at[lax.rem(y + d, NY)], xb_r.at[d - 1], place(d, 0, 0, 0)) for d in STEPS_4]

    for copy in meta_z_copies:
        copy.wait_recv()
    lane_tile = iota((8, 128), 1) // CAP
    numbers = jnp.where(lane_tile == 0, meta_z[...], 0.0)
    for d in range(1, NZ):
        numbers += jnp.where(lane_tile == d, meta_2[d], 0.0)
    numbers = jnp.where(lane_tile < NZ, numbers, 0.0).astype(BF16)
    spread_r, spread_c = iota((128, SEQ), 0), iota((128, SEQ), 1)
    spread = (spread_r // CAP == spread_c // 16) & (lax.rem(spread_r, CAP) == lax.rem(spread_c, CAP))
    where_s[...] = dot_nn(numbers, spread.astype(BF16))

    def add_rows(lane):
        hits = (rows_i.astype(F32) == where_s[lane : lane + 1, :]).astype(BF16)
        rows = jnp.concatenate([lane_s[lane, 0:1], far_s[lane, 1:NZ]], axis=0).reshape(SEQ, 128)
        quarter = lax.rem(iota((SEQ, 128), 0), 16) // CAP
        wide = jnp.concatenate([jnp.where(quarter == j, rows, zero) for j in range(4)], axis=1)
        return dot_nn(hits, wide).reshape(4, 64, D)

    def add_group(group):
        for copy in far_copies[group]:
            copy.wait_recv()
        for lane in range(*GROUPS[group]):
            if lane:
                total_s[...] += add_rows(lane)
            else:
                total_s[...] = add_rows(lane)

    add_group(0)
    add_group(1)

    for copy in (*xa_copies, *xb_copies):
        copy.wait_recv()
    a_sum = dw_own[0, :, pl.ds(x, 1)].reshape(4, 128, 128)
    b_sum = dw_own[1, pl.ds(y, 1)].reshape(4, 128, 128)
    for i in range(3):
        a_sum += xa_r[i].astype(F32)
        b_sum += xb_r[i].astype(F32)
    a_own[...] = a_sum
    b_own[...] = b_sum
    ya_s[...] = a_sum.astype(BF16)
    yb_s[...] = b_sum.astype(BF16)
    ya_copies = [remote(ya_s.at[lax.rem(y + d, NY)], ya_r.at[d - 1], place(d, 0, 0, 0)) for d in STEPS_4]
    yb_copies = [remote(yb_s.at[lax.rem(x + d, NX)], yb_r.at[d - 1], place(0, d, 0, 0)) for d in STEPS_4]

    add_group(2)

    for copy in (*ya_copies, *yb_copies):
        copy.wait_recv()
    a_end, b_end = a_own[y], b_own[x]
    for i in range(3):
        a_end += ya_r[i].astype(F32)
        b_end += yb_r[i].astype(F32)
    tiles = jnp.concatenate([a_end.reshape(NZ, 8, 128), b_end.reshape(NZ, 8, 128)], axis=1)
    zt_own[...] = tiles
    zt_s[...] = tiles.astype(BF16)

    add_group(3)
    add_group(4)

    ty_s[...] = total_s[...].astype(BF16)
    ty_copies = [remote(ty_s.at[lax.rem(y + d, NY)], ty_r.at[d - 1], place(d, 0, 0, 0)) for d in STEPS_4]
    zt_copies = [remote(zt_s.at[lax.rem(z + d, NZ)], zt_r.at[d - 1], place(0, 0, d, 0)) for d in STEPS_Z]
    for copy in ty_copies:
        copy.wait_recv()
    quarter_sum = total_s[y]
    for i in range(3):
        quarter_sum += ty_r[i].astype(F32)
    tg_s[...] = quarter_sum.astype(BF16)
    tg_copies = {d: remote(tg_s, tg_r.at[d - 1], place(d, 0, 0, 0)) for d in STEPS_4}
    table_ref[pl.ds(pl.multiple_of(y * 64, 64), 64), :] = tg_s[...].astype(F32)

    for copy in zt_copies:
        copy.wait_recv()
    tile = zt_own[z]
    for i in range(NZ - 1):
        tile += zt_r[i].astype(F32)
    fin_s[...] = tile
    fin_copy = remote(fin_s, fin_r, place(0, 0, 0, 1))

    for d, copy in tg_copies.items():
        copy.wait_recv()
        source = lax.rem(y + NY - d, NY)
        table_ref[pl.ds(pl.multiple_of(source * 64, 64), 64), :] = tg_r[d - 1].astype(F32)

    fin_copy.wait_recv()
    mine, theirs = fin_s[...], fin_r[...]
    pieces = []
    for half in range(2):
        block_half = jnp.where(is_first, mine, theirs) if half == 0 else jnp.where(is_first, theirs, mine)
        for part in range(2):
            pieces.append(
                jnp.where(is_first, block_half[8 * part : 8 * part + 4], block_half[8 * part + 4 : 8 * part + 8])
            )
    weight_ref[...] = jnp.concatenate(pieces, axis=1)

    for copy in started:
        copy.wait_send()


def body(history, dout, lengths, item_ids, row_place, w1):
    scratch = [
        pltpu.VMEM((SEQ, D), F32),
        pltpu.VMEM((SEQ, D), BF16),
        pltpu.VMEM((SEQ, 4 * D), BF16),
        pltpu.VMEM((SEQ, 4 * D), F32),
        pltpu.VMEM((HEADS, SEQ, SEQ), BF16),
        pltpu.VMEM((HEADS, SEQ, SEQ), F32),
        pltpu.VMEM((SEQ, D), F32),
        pltpu.VMEM((SEQ, D), BF16),
        pltpu.VMEM((SEQ, 4 * D), BF16),
        pltpu.VMEM((8, SEQ), F32),
        pltpu.VMEM((8, 8, 128), F32),
        pltpu.VMEM((8, 8, 128), F32),
        pltpu.VMEM((8, 128), F32),
        pltpu.VMEM((NZ, 8, 128), F32),
        pltpu.VMEM((8, SEQ), F32),
        pltpu.VMEM((8, NZ, 16, 128), BF16),
        pltpu.VMEM((8, NZ, 16, 128), BF16),
        pltpu.VMEM((8, NZ, 16, 128), BF16),
        pltpu.VMEM((4, 64, D), F32),
        pltpu.VMEM((4, 64, D), BF16),
        pltpu.VMEM((3, 64, D), BF16),
        pltpu.VMEM((64, D), BF16),
        pltpu.VMEM((3, 64, D), BF16),
        pltpu.VMEM((2, 4, 4, 128, 128), F32),
        pltpu.VMEM((2, 4, 4, 128, 128), BF16),
        pltpu.VMEM((2, 4, 4, 128, 128), BF16),
        pltpu.VMEM((4, 4, 128, 128), BF16),
        pltpu.VMEM((3, 4, 128, 128), BF16),
        pltpu.VMEM((4, 4, 128, 128), BF16),
        pltpu.VMEM((3, 4, 128, 128), BF16),
        pltpu.VMEM((4, 128, 128), F32),
        pltpu.VMEM((4, 128, 128), F32),
        pltpu.VMEM((4, 128, 128), BF16),
        pltpu.VMEM((3, 128, 128), BF16),
        pltpu.VMEM((4, 128, 128), BF16),
        pltpu.VMEM((3, 128, 128), BF16),
        pltpu.VMEM((NZ, 16, 128), F32),
        pltpu.VMEM((NZ, 16, 128), BF16),
        pltpu.VMEM((NZ - 1, 16, 128), BF16),
        pltpu.VMEM((16, 128), F32),
        pltpu.VMEM((16, 128), F32),
        pltpu.SemaphoreType.DMA((N_COPIES,)),
        pltpu.SemaphoreType.DMA((N_COPIES,)),
    ]
    vmem = pl.BlockSpec(memory_space=pltpu.VMEM)
    return pl.pallas_call(
        kernel,
        out_shape=(
            jax.ShapeDtypeStruct((SEQ, D), F32),
            jax.ShapeDtypeStruct((4, D), F32),
        ),
        in_specs=[vmem] * 6,
        out_specs=(vmem, vmem),
        scratch_shapes=scratch,
        compiler_params=pltpu.CompilerParams(
            collective_id=0, has_side_effects=True, vmem_limit_bytes=48 * 2**20
        ),
        cost_estimate=pl.CostEstimate(flops=4 * 10**9, bytes_accessed=8 * 10**6, transcendentals=10**6),
    )(history, dout, lengths.reshape(1, 1), item_ids, row_place.reshape(256, 128), w1)


def solution(mesh):
    return jax.shard_map(
        body,
        mesh=mesh,
        in_specs=(
            P(("dp", "emb"), None, None),
            P(("dp", "emb"), None, None),
            P(("dp", "emb")),
            P(("dp", "emb"), None),
            P(),
            P(),
        ),
        out_specs=(P("emb", None), P(("dp", "emb"), None)),
        check_vma=False,
    )
```

time: 657 us -> 69.7 us (0.11)
  waiting for transfers between devices: 531 us -> 0 us
  Pallas kernels: 0 us -> 61.5 us
  starting transfers between devices: 38.4 us -> 0 us
  matrix products: 19.2 us -> 0 us
  other arithmetic: 17.7 us -> 0 us
  local copies, waits for them, and re-layouts: 22.4 us -> 6.46 us
  between operations: 16.6 us -> 1.3 us
  blocking collectives: 9.45 us -> 0 us
    unnamed x3 -> x0, waiting for transfers between devices: 520 us -> none
    pallas_call x0 -> x1, Pallas kernels: none -> 61.5 us  [body(): pl.pallas_call(kernel, out_shape=(jax.ShapeDtypeStruct((SEQ, D), F32), ja...]
    all_to_all x2 -> x0, starting transfers between devices: 38.3 us -> none  [the longest x1 22.2 us: body(): lax.all_to_all(every_target, 'emb', split_axis=0, concat_axis=0, tiled=True)]
    dot_general x10 -> x0, matrix products: 19.2 us -> none  [the longest x1 3.49 us: shard_sum(): lax.dot_general(onehot, flat_rows, (((0,), (0,)), ((), ())), preferred_el...]
    all_gather x1 -> x0, waiting for transfers between devices: 9.88 us -> none  [body(): every_row = lax.all_gather(outgoing, 'dp', axis=1, tiled=True)]
    all_gather x1 -> x0, blocking collectives: 9.45 us -> none  [body(): every_target = lax.all_gather(targets, 'dp', axis=1, tiled=True)]
    reshape x7 -> x0, local copies, waits for them, and re-layouts: 8.25 us -> none  [the longest x2 3.89 us: body(): outgoing = jnp.zeros((group * capacity, width), jnp.bfloat16).at[slot].se...]
  transfers between devices with their start and end apart: 4 -> 0, of which waited for: 3 -> 0; matrix products, arithmetic and copies ran while one was open for 2% -> 0% of each run, Pallas kernels for 0% -> 0%
where the time goes in v1:
time: 69.7 us; the launch traced here: 69.3 us
  Pallas kernels  61.5 us (88%)
  local copies, waits for them, and re-layouts  6.46 us (9%)
  between operations  1.3 us (2%)
    pallas_call x1, Pallas kernels, body(): pl.pallas_call(kernel, out_shape=(jax.ShapeDtypeStruct((SEQ, D), F32), ja...  61.5 us
    unnamed x12, local copies, waits for them, and re-layouts  6.46 us

profile of v1, /device:TPU:1, one launch (start us, length us, event | category | flops | bytes accessed | tf_op | source)
XLA Modules:
  0.0 69.3 jit_solution(3578317903334471751)
XLA Ops:
  1.3 0.0 copy-start
  1.3 1.6 %copy-done = bf16[2048,512]{1,0:T(8,128)(2,1)S(1)} copy-done((bf16[2048,512]{1,0:T(8,128)(2,1)S(1)}, bf16[2048,512]{1,0:T(8,128)(2,1)}, u32[]{:S(2)}) %copy-start) | copy-done | bytes 2097176
  2.9 0.0 copy-start.1
  2.9 0.9 %copy-done.1 = bf16[1,256,512]{2,1,0:T(8,128)(2,1)S(1)} copy-done((bf16[1,256,512]{2,1,0:T(8,128)(2,1)S(1)}, bf16[1,256,512]{2,1,0:T(8,128)(2,1)}, u32[]{:S(2)}) %copy-start.1) | copy-done | bytes 262168
  3.8 0.0 copy-start.2
  3.8 0.9 %copy-done.2 = bf16[1,256,512]{2,1,0:T(8,128)(2,1)S(1)} copy-done((bf16[1,256,512]{2,1,0:T(8,128)(2,1)S(1)}, bf16[1,256,512]{2,1,0:T(8,128)(2,1)}, u32[]{:S(2)}) %copy-start.2) | copy-done | bytes 262168
  4.8 0.0 copy-start.3
  4.8 0.9 %copy-done.3 = s32[32768]{0:T(1024)S(1)} copy-done((s32[32768]{0:T(1024)S(1)}, s32[32768]{0:T(1024)}, u32[]{:S(2)}) %copy-start.3) | copy-done | bytes 131096
  5.7 0.0 copy-start.4
  5.7 0.7 copy-done.4
  6.4 61.5 %shard_map.77 = (f32[256,512]{1,0:T(8,128)S(1)}, f32[4,512]{1,0:T(4,128)S(1)}) custom-call(bf16[1,256,512]{2,1,0:T(8,128)(2,1)S(1)} %copy-done.1, bf16[1,256,512]{2,1,0:T(8,128)(2,1)S(1)} %copy-done.2, s32[1,1]{1,0:T(1,128)} %bitcast.2.len_ref, s32[1,256]{1,0:T(1,128)S(1)} %copy-done.4, s32[256,128]{1,0:T(8,128)S(1)} %bitcast.3, bf16[2048,512]{1,0:T(8,128)(2,1)S(1)} %copy-done), custom_call_target="tpu_custom_call" | custom-call | flops 4000000000 | bytes 8000000 | tf_op jit(solution)/shard_map/pallas_call | solution.py:447
  67.9 0.8 %copy.11 = f32[256,512]{1,0:T(8,128)} copy(f32[256,512]{1,0:T(8,128)S(1)} %get-tuple-element.4) | data formatting | bytes 1048576
  68.7 0.6 copy.12
Async XLA Ops:
  1.3 1.6 %copy-start = (bf16[2048,512]{1,0:T(8,128)(2,1)S(1)}, bf16[2048,512]{1,0:T(8,128)(2,1)}, u32[]{:S(2)}) copy-start(bf16[2048,512]{1,0:T(8,128)(2,1)} %w1_ref.1) | copy-start | bytes 6291460
  2.9 0.9 %copy-start.1 = (bf16[1,256,512]{2,1,0:T(8,128)(2,1)S(1)}, bf16[1,256,512]{2,1,0:T(8,128)(2,1)}, u32[]{:S(2)}) copy-start(bf16[1,256,512]{2,1,0:T(8,128)(2,1)} %hist_ref.1) | copy-start | bytes 786436
  3.8 0.9 %copy-start.2 = (bf16[1,256,512]{2,1,0:T(8,128)(2,1)S(1)}, bf16[1,256,512]{2,1,0:T(8,128)(2,1)}, u32[]{:S(2)}) copy-start(bf16[1,256,512]{2,1,0:T(8,128)(2,1)} %dout_ref.1) | copy-start | bytes 786436
  4.8 0.9 %copy-start.3 = (s32[32768]{0:T(1024)S(1)}, s32[32768]{0:T(1024)}, u32[]{:S(2)}) copy-start(s32[32768]{0:T(1024)} %param.10) | copy-start | bytes 393220
  5.7 0.7 copy-start.4

commit v2 on v1

--- a/solution.py
+++ b/solution.py
@@ -20,7 +20,8 @@
 
 LANES = tuple((xs, cs) for xs in (0, 1, 3, 2) for cs in (0, 1))
 GROUPS = ((0, 1), (1, 2), (2, 4), (4, 6), (6, 8))
-STEPS_Z = tuple(sorted(range(1, NZ), key=lambda d: -min(d, NZ - d)))
+NEAR = (3, -3, 2, -2, 1, -1)
+RELAY = 4
 STEPS_4 = (2, 1, 3)
 
 
@@ -79,18 +80,19 @@
         return made
 
 
-N_COPIES = 7 + 15 + 7 + 15 * len(GROUPS) + 1 + 6 + 6 + 15 + 1 + 3 + 3
+N_COPIES = 31 + 31 + 13 * len(GROUPS) + 14 + 2 + 3 + 1 + 6 + 6 + 13 + 2 + 1
 
 
 def kernel(
-    hist_ref, dout_ref, len_ref, ids_ref, place_ref, w1_ref,
+    hist_any, dout_any, len_ref, ids_any, place_any, w1_any,
     table_ref, weight_ref,
+    hist_ref, dout_ref, ids_ref, place_ref, w1_ref,
     xnorm, xn, act, slope, probs, sslope, attn, d_o, d_g,
-    slot_s, meta_s, meta_1, meta_z, meta_2, where_s,
-    out_s, lane_s, far_s, total_s, ty_s, ty_r, tg_s, tg_r,
+    slot_s, meta_s, meta_1, meta_z, meta_near, meta_relay,
+    out_s, lane_s, z_s, near_r, relay_r, sum_s, sum_r, tg_s, tg_r,
     dw_own, dw_s, dw_r, xa_s, xa_r, xb_s, xb_r, a_own, b_own, ya_s, ya_r, yb_s, yb_r,
-    zt_own, zt_s, zt_r, fin_s, fin_r,
-    send, recv,
+    zt_own, zt_s, zt_near, zt_relay, zt_far, zt_sum_s, zt_sum_r, fin_s, fin_r,
+    load, send, recv,
 ):
     y = lax.axis_index("dp")
     emb = lax.axis_index("emb")
@@ -101,15 +103,21 @@
     def place(dy, dx, dz, dc):
         return (
             lax.rem(y + dy, NY),
-            (lax.rem(x + dx, NX) * NZ + lax.rem(z + dz, NZ)) * NC + lax.rem(c + dc, NC),
+            (lax.rem(x + dx, NX) * NZ + lax.rem(z + dz + NZ, NZ)) * NC + lax.rem(c + dc, NC),
         )
 
-    partners = [place(0, xs, 0, cs) for xs, cs in LANES[1:]]
-    partners += [place(0, 0, d, 0) for d in STEPS_Z]
-    partners += [place(d, 0, 0, 0) for d in STEPS_4]
+    partners = [place(0, 0, d, 0) for d in (RELAY, -RELAY, *NEAR)]
+    partners += [place(d, xs, 0, cs) for xs, cs in LANES for d in range(NY) if d or xs or cs]
     barrier = pltpu.get_barrier_semaphore()
     for partner in partners:
         pl.semaphore_signal(barrier, inc=1, device_id=partner, device_id_type=MESH)
+
+    sources = [(ids_any, ids_ref), (place_any, place_ref), (hist_any, hist_ref)]
+    sources += [(w1_any.at[pl.ds(D * i, D)], w1_ref.at[pl.ds(D * i, D)]) for i in range(4)]
+    sources += [(dout_any, dout_ref)]
+    loads = [pltpu.make_async_copy(src, dst, load.at[i]) for i, (src, dst) in enumerate(sources)]
+    for copy in loads:
+        copy.start()
 
     sems = Sems(send, recv)
     started = []
@@ -121,6 +129,8 @@
 
     rows_i, cols_i = iota((SEQ, SEQ), 0), iota((SEQ, SEQ), 1)
     eye = rows_i == cols_i
+    loads[0].wait()
+    loads[1].wait()
     ids_row = ids_ref[...].astype(F32)
     ids = jnp.sum(jnp.where(eye, ids_row, 0.0), axis=1, keepdims=True).astype(jnp.int32)
     high = (cols_i == ids // 128).astype(BF16)
@@ -145,19 +155,20 @@
         wanted = (lane128 + lane * NZ * CAP).astype(F32)
         hit = (slot == wanted) & (lane128 < NZ * CAP)
         found = jnp.sum(jnp.where(hit, local - 256.0, 0.0), axis=0, keepdims=True) + 256.0
-        meta = jnp.broadcast_to(found, (8, 128))
-        if lane:
-            meta_s[lane] = meta
-        else:
-            meta_1[0] = meta
+        meta_s[lane] = found
+        if lane == 0:
+            meta_1[0, 0] = found
 
     length = len_ref[...]
     inverse_len = 1.0 / length.astype(F32)
     valid = iota((SEQ, 1), 0) < length
+    loads[2].wait()
     normed, rstd_x = layer_norm(hist_ref[0].astype(F32))
     xnorm[...] = normed
     xn[...] = normed.astype(BF16)
     for at in range(0, 4 * D, 256):
+        if at % D == 0:
+            loads[3 + at // D].wait()
         gate = dot_nt(xn[...], w1_ref[at : at + 256, :])
         value, slant = silu_and_slope(gate)
         act[:, at : at + 256] = value.astype(BF16)
@@ -187,20 +198,13 @@
             total = term if total is None else total + term
         attn[:, at : at + 128] = total
 
-    pl.semaphore_wait(barrier, len(partners))
-    meta_copies = {
-        lane: remote(meta_s.at[lane], meta_1.at[lane], place(0, xs, 0, cs))
-        for lane, (xs, cs) in enumerate(LANES)
-        if lane
-    }
-
     o_norm, rstd_o = layer_norm(attn[...])
+    loads[7].wait()
     dy = jnp.where(valid, dout_ref[0].astype(F32), 0.0)
     d_g[:, :D] = (dy * o_norm * slope[:, :D]).astype(BF16)
     d_on = dy * act[:, :D].astype(F32)
     d_o[...] = norm_back(d_on, o_norm, rstd_o).astype(BF16)
 
-    meta_z_copies = []
     for pair in range(HEADS // 2):
         at = pair * 128
         v = act[:, D + at : D + at + 128]
@@ -223,53 +227,60 @@
         for part, grad in enumerate((d_v, d_q, d_k), 1):
             cols = slice(part * D + at, part * D + at + 128)
             d_g[:, cols] = (grad * slope[:, cols]).astype(BF16)
-        if pair == 2:
-            tile_row = iota((8, 128), 0)
-            gathered = jnp.where(tile_row == 0, meta_1[0], 0.0)
-            for lane, copy in meta_copies.items():
-                copy.wait_recv()
-                gathered += jnp.where(tile_row == lane, meta_1[lane], 0.0)
-            meta_z[...] = gathered
-            meta_z_copies = [remote(meta_z, meta_2.at[d], place(0, 0, d, 0)) for d in STEPS_Z]
 
     d_xn = dot_nn(d_g[...], w1_ref[...])
     d_x = norm_back(d_xn, xnorm[...], rstd_x) + dy
     d_x = jnp.where(valid, d_x, 0.0).astype(BF16)
 
-    def pack(lane):
-        line = iota((SEQ, SEQ), 0)
-        wanted = (line // 16) * CAP + lax.rem(line, CAP) + lane * NZ * CAP
+    for lane in range(8):
+        wanted = iota((64, SEQ), 0) + lane * NZ * CAP
         pick = (wanted.astype(F32) == slot_s[0:1, :]).astype(BF16)
-        moved = dot_nn(pick, d_x)
-        quarter = lax.rem(iota((SEQ, 128), 0), 16) // CAP
-        rows = moved[:, 0:128]
-        for j in range(1, 4):
-            rows = jnp.where(quarter == j, moved[:, 128 * j : 128 * j + 128], rows)
-        return rows.astype(BF16).reshape(NZ, 16, 128)
-
-    far_copies = [None] * len(GROUPS)
+        moved = dot_nn(pick, d_x).astype(BF16)
+        for q in range(NY):
+            out_s[lane, q] = moved[:, 128 * q : 128 * q + 128]
+
+    pl.semaphore_wait(barrier, len(partners))
+    meta_copies, lane_copies = {}, {}
+
+    def to_lanes(*lanes):
+        for lane in lanes:
+            xs, cs = LANES[lane]
+            meta_copies[lane], lane_copies[lane] = [], []
+            for d in (2, 1, 3, 0):
+                if lane or d:
+                    there = place(d, xs, 0, cs)
+                    meta_copies[lane].append(remote(meta_s.at[lane], meta_1.at[lane, d], there))
+                    lane_copies[lane].append(remote(out_s.at[lane, lax.rem(y + d, NY)], lane_s.at[lane, d], there))
+
+    to_lanes(*range(8))
+    lane_s[0, 0] = out_s[0, y]
+
+    to_r, from_r = iota((SEQ, SEQ), 0), iota((SEQ, SEQ), 1)
+    order = (to_r // 16 == lax.rem(from_r, 64) // CAP) & (lax.rem(to_r, 16) // CAP == from_r // 64)
+    order = (order & (lax.rem(to_r, CAP) == lax.rem(from_r, CAP))).astype(BF16)
+    near_copies, relay_copies = [], ([], [])
 
     def pass_on(group):
-        low_lane, high_lane = GROUPS[group]
-        far_copies[group] = [
-            remote(
-                lane_s.at[pl.ds(low_lane, high_lane - low_lane), d],
-                far_s.at[pl.ds(low_lane, high_lane - low_lane), d],
-                place(0, 0, d, 0),
-            )
-            for d in STEPS_Z
-        ]
-
-    lane_copies = {}
-    lane_s[0] = pack(0)
-    pass_on(0)
-    for lane in (1, 6, 7, 2, 3, 4, 5):
-        xs, cs = LANES[lane]
-        out_s[lane] = pack(lane)
-        lane_copies[lane] = remote(out_s.at[lane], lane_s.at[lane], place(0, xs, 0, cs))
+        low, high = GROUPS[group]
+        for lane in range(low, high):
+            for copy in lane_copies[lane]:
+                copy.wait_recv()
+            rows = dot_nn(order, lane_s[lane].reshape(SEQ, 128)).astype(BF16)
+            z_s[:, lane] = rows.reshape(NZ, 16, 128)
+        lanes = pl.ds(low, high - low)
+        way = 0 if low < 4 else 1
+        ahead = (RELAY, -RELAY)[way]
+        relay_copies[way].append(remote(z_s.at[8, lanes], relay_r.at[way, 3, lanes], place(0, 0, ahead, 0)))
+        for d in NEAR:
+            way = 0 if d > 0 else 1
+            far = (d + (RELAY, -RELAY)[way]) % NZ
+            relay_copies[way].append(remote(z_s.at[far, lanes], relay_r.at[way, abs(d) - 1, lanes], place(0, 0, d, 0)))
+        for at, d in enumerate(NEAR):
+            near_copies.append(remote(z_s.at[d % NZ, lanes], near_r.at[at, lanes], place(0, 0, d, 0)))
 
     is_first = c == 0
-    for block_at in range(8):
+
+    def share_of_weight(block_at):
         share = dot_tn(d_g[:, 256 * block_at : 256 * block_at + 256], xn[...])
         left, right = share[:, :256], share[:, 256:]
         own = jnp.where(is_first, left, right)
@@ -280,13 +291,37 @@
                 to = 2 * block_at + sub
                 dw_own[part, to // 4, to % 4] = own[cut]
                 dw_s[part, to // 4, to % 4] = other[cut]
+
+    for block_at in range(4):
+        share_of_weight(block_at)
+    pass_on(0)
+    for block_at in range(4, 8):
+        share_of_weight(block_at)
     dw_copy = remote(dw_s, dw_r, place(0, 0, 0, 1))
-
-    lane_copies[1].wait_recv()
     pass_on(1)
+
+    for lane in range(8):
+        for copy in meta_copies[lane]:
+            copy.wait_recv()
+    same_rank = lax.rem(iota((128, 128), 0), CAP) == lax.rem(iota((128, 128), 1), CAP)
+    tall = jnp.concatenate([meta_1[lane, d] for lane in range(8) for d in range(NY)], axis=0)
+    tall = jnp.broadcast_to(tall[None], (NZ, 32, 128))
+    tall = jnp.where(iota((NZ, 32, 128), 2) // CAP == iota((NZ, 32, 128), 0), tall, 0.0)
+    lines = dot_nn(tall.reshape(512, 128).astype(BF16), same_rank.astype(BF16)).reshape(NZ, 32, 128)
+    lines = jnp.where(iota((NZ, 32, 128), 2) // CAP == iota((NZ, 32, 128), 1), lines, 0.0)
+    lines = jnp.sum(lines, axis=1)
+    for d in range(NZ):
+        meta_z[d] = lines[d : d + 1]
+    meta_z_copies = []
+    for way, ahead in enumerate((RELAY, -RELAY)):
+        meta_z_copies.append(remote(meta_z.at[8], meta_relay.at[way, 3], place(0, 0, ahead, 0)))
+    for at, d in enumerate(NEAR):
+        way = 0 if d > 0 else 1
+        far = (d + (RELAY, -RELAY)[way]) % NZ
+        meta_z_copies.append(remote(meta_z.at[far], meta_relay.at[way, abs(d) - 1], place(0, 0, d, 0)))
+        meta_z_copies.append(remote(meta_z.at[d % NZ], meta_near.at[at], place(0, 0, d, 0)))
+
     for group in (2, 3, 4):
-        for lane in range(*GROUPS[group]):
-            lane_copies[lane].wait_recv()
         pass_on(group)
 
     dw_copy.wait_recv()
@@ -298,35 +333,25 @@
     xa_copies = [remote(xa_s.at[:, lax.rem(x + d, NX)], xa_r.at[d - 1], place(0, d, 0, 0)) for d in STEPS_4]
     xb_copies = [remote(xb_s.at[lax.rem(y + d, NY)], xb_r.at[d - 1], place(d, 0, 0, 0)) for d in STEPS_4]
 
+    row_of = iota((SEQ, 128), 0).astype(F32)
+
+    def add_up(lines_and_rows):
+        hits = jnp.concatenate([(row_of == line).astype(BF16) for line, _ in lines_and_rows], axis=1)
+        return dot_nn(hits, jnp.concatenate([rows for _, rows in lines_and_rows], axis=0))
+
     for copy in meta_z_copies:
         copy.wait_recv()
-    lane_tile = iota((8, 128), 1) // CAP
-    numbers = jnp.where(lane_tile == 0, meta_z[...], 0.0)
-    for d in range(1, NZ):
-        numbers += jnp.where(lane_tile == d, meta_2[d], 0.0)
-    numbers = jnp.where(lane_tile < NZ, numbers, 0.0).astype(BF16)
-    spread_r, spread_c = iota((128, SEQ), 0), iota((128, SEQ), 1)
-    spread = (spread_r // CAP == spread_c // 16) & (lax.rem(spread_r, CAP) == lax.rem(spread_c, CAP))
-    where_s[...] = dot_nn(numbers, spread.astype(BF16))
-
-    def add_rows(lane):
-        hits = (rows_i.astype(F32) == where_s[lane : lane + 1, :]).astype(BF16)
-        rows = jnp.concatenate([lane_s[lane, 0:1], far_s[lane, 1:NZ]], axis=0).reshape(SEQ, 128)
-        quarter = lax.rem(iota((SEQ, 128), 0), 16) // CAP
-        wide = jnp.concatenate([jnp.where(quarter == j, rows, zero) for j in range(4)], axis=1)
-        return dot_nn(hits, wide).reshape(4, 64, D)
-
-    def add_group(group):
-        for copy in far_copies[group]:
+    none = jnp.zeros((64, 128), BF16)
+    sum_copies = []
+    for way, ahead in enumerate((RELAY, -RELAY)):
+        for copy in relay_copies[way]:
             copy.wait_recv()
-        for lane in range(*GROUPS[group]):
-            if lane:
-                total_s[...] += add_rows(lane)
-            else:
-                total_s[...] = add_rows(lane)
-
-    add_group(0)
-    add_group(1)
+        half = relay_r[way, 3, 4 * way : 4 * way + 4].reshape(64, 128)
+        terms = [(meta_z[ahead % NZ], z_s[ahead % NZ].reshape(128, 128))]
+        terms += [(meta_relay[way, i], relay_r[way, i].reshape(128, 128)) for i in range(3)]
+        terms += [(meta_relay[way, 3], jnp.concatenate([none, half] if way else [half, none], axis=0))]
+        sum_s[way] = add_up(terms).astype(BF16)
+        sum_copies.append(remote(sum_s.at[way], sum_r.at[way], place(0, 0, ahead, 0)))
 
     for copy in (*xa_copies, *xb_copies):
         copy.wait_recv()
@@ -342,7 +367,11 @@
     ya_copies = [remote(ya_s.at[lax.rem(y + d, NY)], ya_r.at[d - 1], place(d, 0, 0, 0)) for d in STEPS_4]
     yb_copies = [remote(yb_s.at[lax.rem(x + d, NX)], yb_r.at[d - 1], place(0, d, 0, 0)) for d in STEPS_4]
 
-    add_group(2)
+    for copy in near_copies:
+        copy.wait_recv()
+    table = add_up(
+        [(meta_z[0], z_s[0].reshape(128, 128))] + [(meta_near[i], near_r[i].reshape(128, 128)) for i in range(6)]
+    )
 
     for copy in (*ya_copies, *yb_copies):
         copy.wait_recv()
@@ -354,34 +383,45 @@
     zt_own[...] = tiles
     zt_s[...] = tiles.astype(BF16)
 
-    add_group(3)
-    add_group(4)
-
-    ty_s[...] = total_s[...].astype(BF16)
-    ty_copies = [remote(ty_s.at[lax.rem(y + d, NY)], ty_r.at[d - 1], place(d, 0, 0, 0)) for d in STEPS_4]
-    zt_copies = [remote(zt_s.at[lax.rem(z + d, NZ)], zt_r.at[d - 1], place(0, 0, d, 0)) for d in STEPS_Z]
-    for copy in ty_copies:
-        copy.wait_recv()
-    quarter_sum = total_s[y]
-    for i in range(3):
-        quarter_sum += ty_r[i].astype(F32)
-    tg_s[...] = quarter_sum.astype(BF16)
+
+    zt_copies = [remote(zt_s.at[lax.rem(z + 8, NZ)], zt_far, place(0, 0, RELAY + 8 * c, 0))]
+    for at, d in enumerate(NEAR):
+        way = 0 if d > 0 else 1
+        far = (d + (RELAY, -RELAY)[way]) % NZ
+        zt_copies.append(
+            remote(zt_s.at[lax.rem(z + far, NZ)], zt_relay.at[way, abs(d) - 1], place(0, 0, d, 0))
+        )
+        zt_copies.append(remote(zt_s.at[lax.rem(z + d % NZ, NZ)], zt_near.at[at], place(0, 0, d, 0)))
+
+    for copy in sum_copies:
+        copy.wait_recv()
+    tg_s[...] = (table + (sum_r[0].astype(F32) + sum_r[1].astype(F32))).astype(BF16)
     tg_copies = {d: remote(tg_s, tg_r.at[d - 1], place(d, 0, 0, 0)) for d in STEPS_4}
-    table_ref[pl.ds(pl.multiple_of(y * 64, 64), 64), :] = tg_s[...].astype(F32)
+    table_ref[:, pl.ds(pl.multiple_of(y * 128, 128), 128)] = tg_s[...].astype(F32)
 
     for copy in zt_copies:
         copy.wait_recv()
+    zt_sum_copies = []
+    for way, ahead in enumerate((RELAY, -RELAY)):
+        tile = zt_own[lax.rem(z + ahead % NZ, NZ)] + jnp.where(c == way, zt_far[...].astype(F32), 0.0)
+        for i in range(3):
+            tile += zt_relay[way, i].astype(F32)
+        zt_sum_s[way] = tile.astype(BF16)
+        zt_sum_copies.append(remote(zt_sum_s.at[way], zt_sum_r.at[way], place(0, 0, ahead, 0)))
     tile = zt_own[z]
-    for i in range(NZ - 1):
-        tile += zt_r[i].astype(F32)
+    for i in range(6):
+        tile += zt_near[i].astype(F32)
+
+    for d, copy in tg_copies.items():
+        copy.wait_recv()
+        source = lax.rem(y + NY - d, NY)
+        table_ref[:, pl.ds(pl.multiple_of(source * 128, 128), 128)] = tg_r[d - 1].astype(F32)
+
+    for way, copy in enumerate(zt_sum_copies):
+        copy.wait_recv()
+        tile += zt_sum_r[way].astype(F32)
     fin_s[...] = tile
     fin_copy = remote(fin_s, fin_r, place(0, 0, 0, 1))
-
-    for d, copy in tg_copies.items():
-        copy.wait_recv()
-        source = lax.rem(y + NY - d, NY)
-        table_ref[pl.ds(pl.multiple_of(source * 64, 64), 64), :] = tg_r[d - 1].astype(F32)
-
     fin_copy.wait_recv()
     mine, theirs = fin_s[...], fin_r[...]
     pieces = []
@@ -399,6 +439,11 @@
 
 def body(history, dout, lengths, item_ids, row_place, w1):
     scratch = [
+        pltpu.VMEM((1, SEQ, D), BF16),
+        pltpu.VMEM((1, SEQ, D), BF16),
+        pltpu.VMEM((1, SEQ), jnp.int32),
+        pltpu.VMEM((256, 128), jnp.int32),
+        pltpu.VMEM((4 * D, D), BF16),
         pltpu.VMEM((SEQ, D), F32),
         pltpu.VMEM((SEQ, D), BF16),
         pltpu.VMEM((SEQ, 4 * D), BF16),
@@ -409,19 +454,20 @@
         pltpu.VMEM((SEQ, D), BF16),
         pltpu.VMEM((SEQ, 4 * D), BF16),
         pltpu.VMEM((8, SEQ), F32),
-        pltpu.VMEM((8, 8, 128), F32),
-        pltpu.VMEM((8, 8, 128), F32),
-        pltpu.VMEM((8, 128), F32),
-        pltpu.VMEM((NZ, 8, 128), F32),
-        pltpu.VMEM((8, SEQ), F32),
-        pltpu.VMEM((8, NZ, 16, 128), BF16),
-        pltpu.VMEM((8, NZ, 16, 128), BF16),
-        pltpu.VMEM((8, NZ, 16, 128), BF16),
-        pltpu.VMEM((4, 64, D), F32),
-        pltpu.VMEM((4, 64, D), BF16),
-        pltpu.VMEM((3, 64, D), BF16),
-        pltpu.VMEM((64, D), BF16),
-        pltpu.VMEM((3, 64, D), BF16),
+        pltpu.VMEM((8, 1, 128), F32),
+        pltpu.VMEM((8, NY, 1, 128), F32),
+        pltpu.VMEM((NZ, 1, 128), F32),
+        pltpu.VMEM((6, 1, 128), F32),
+        pltpu.VMEM((2, 4, 1, 128), F32),
+        pltpu.VMEM((8, NY, 64, 128), BF16),
+        pltpu.VMEM((8, NY, 64, 128), BF16),
+        pltpu.VMEM((NZ, 8, 16, 128), BF16),
+        pltpu.VMEM((6, 8, 16, 128), BF16),
+        pltpu.VMEM((2, 4, 8, 16, 128), BF16),
+        pltpu.VMEM((2, SEQ, 128), BF16),
+        pltpu.VMEM((2, SEQ, 128), BF16),
+        pltpu.VMEM((SEQ, 128), BF16),
+        pltpu.VMEM((3, SEQ, 128), BF16),
         pltpu.VMEM((2, 4, 4, 128, 128), F32),
         pltpu.VMEM((2, 4, 4, 128, 128), BF16),
         pltpu.VMEM((2, 4, 4, 128, 128), BF16),
@@ -437,24 +483,30 @@
         pltpu.VMEM((3, 128, 128), BF16),
         pltpu.VMEM((NZ, 16, 128), F32),
         pltpu.VMEM((NZ, 16, 128), BF16),
-        pltpu.VMEM((NZ - 1, 16, 128), BF16),
+        pltpu.VMEM((6, 16, 128), BF16),
+        pltpu.VMEM((2, 3, 16, 128), BF16),
+        pltpu.VMEM((16, 128), BF16),
+        pltpu.VMEM((2, 16, 128), BF16),
+        pltpu.VMEM((2, 16, 128), BF16),
         pltpu.VMEM((16, 128), F32),
         pltpu.VMEM((16, 128), F32),
+        pltpu.SemaphoreType.DMA((8,)),
         pltpu.SemaphoreType.DMA((N_COPIES,)),
         pltpu.SemaphoreType.DMA((N_COPIES,)),
     ]
     vmem = pl.BlockSpec(memory_space=pltpu.VMEM)
+    hbm = pl.BlockSpec(memory_space=pltpu.HBM)
     return pl.pallas_call(
         kernel,
         out_shape=(
             jax.ShapeDtypeStruct((SEQ, D), F32),
             jax.ShapeDtypeStruct((4, D), F32),
         ),
-        in_specs=[vmem] * 6,
+        in_specs=[hbm, hbm, vmem, hbm, hbm, hbm],
         out_specs=(vmem, vmem),
         scratch_shapes=scratch,
         compiler_params=pltpu.CompilerParams(
-            collective_id=0, has_side_effects=True, vmem_limit_bytes=48 * 2**20
+            collective_id=0, has_side_effects=True, vmem_limit_bytes=63 * 2**20 + 2**19
         ),
         cost_estimate=pl.CostEstimate(flops=4 * 10**9, bytes_accessed=8 * 10**6, transcendentals=10**6),
     )(history, dout, lengths.reshape(1, 1), item_ids, row_place.reshape(256, 128), w1)

time: 69.7 us -> 64.5 us (0.925)
  local copies, waits for them, and re-layouts: 6.46 us -> 3.16 us
  Pallas kernels: 61.5 us -> 59.9 us
    unnamed x12 -> x2, local copies, waits for them, and re-layouts: 6.46 us -> 3.16 us
    pallas_call x1, Pallas kernels: 61.5 us -> 59.9 us  [body(): pl.pallas_call(kernel, out_shape=(jax.ShapeDtypeStruct((SEQ, D), F32), ja...]
where the time goes in v2:
time: 64.5 us; the launch traced here: 64.3 us
  Pallas kernels  59.9 us (93%)
  local copies, waits for them, and re-layouts  3.16 us (5%)
  between operations  1.28 us (2%)
    pallas_call x1, Pallas kernels, body(): pl.pallas_call(kernel, out_shape=(jax.ShapeDtypeStruct((SEQ, D), F32), ja...  59.9 us
    unnamed x2, local copies, waits for them, and re-layouts  3.16 us

profile of v2, /device:TPU:1, one launch (start us, length us, event | category | flops | bytes accessed | tf_op | source)
XLA Modules:
  0.0 64.3 jit_solution(9563369983250733240)
XLA Ops:
  1.3 59.9 %shard_map.77 = (f32[256,512]{1,0:T(8,128)}, f32[4,512]{1,0:T(4,128)}) custom-call(bf16[1,256,512]{2,1,0:T(8,128)(2,1)} %hist_any.1, bf16[1,256,512]{2,1,0:T(8,128)(2,1)} %dout_any.1, s32[1,1]{1,0:T(1,128)} %bitcast.2.len_ref, s32[1,256]{1,0:T(1,128)} %ids_any.1, s32[256,128]{1,0:T(8,128)} %bitcast.3, bf16[2048,512]{1,0:T(8,128)(2,1)} %w1_any.1), custom_call_target="tpu_custom_call" | custom-call | flops 4000000000 | bytes 8000000 | tf_op jit(solution)/shard_map/pallas_call | solution.py:499
  61.1 1.9 %copy.11 = f32[256,512]{1,0:T(8,128)} copy(f32[256,512]{1,0:T(8,128)} %get-tuple-element.4) | data formatting | bytes 1048576
  63.0 1.3 %copy.12 = f32[4,512]{1,0:T(4,128)} copy(f32[4,512]{1,0:T(4,128)} %get-tuple-element.5) | data formatting | bytes 16384

commit v3 on v2

--- a/solution.py
+++ b/solution.py
@@ -27,6 +27,14 @@
 
 def iota(shape, dim):
     return lax.broadcasted_iota(jnp.int32, shape, dim)
+
+
+def part_of(value, size):
+    return lax.shift_right_logical(value, jnp.full(value.shape, size.bit_length() - 1, value.dtype))
+
+
+def rest_of(value, size):
+    return value & (size - 1)
 
 
 def dot_nn(a, b):
@@ -112,9 +120,9 @@
     for partner in partners:
         pl.semaphore_signal(barrier, inc=1, device_id=partner, device_id_type=MESH)
 
-    sources = [(ids_any, ids_ref), (place_any, place_ref), (hist_any, hist_ref)]
+    sources = [(hist_any, hist_ref)]
     sources += [(w1_any.at[pl.ds(D * i, D)], w1_ref.at[pl.ds(D * i, D)]) for i in range(4)]
-    sources += [(dout_any, dout_ref)]
+    sources += [(ids_any, ids_ref), (place_any, place_ref), (dout_any, dout_ref)]
     loads = [pltpu.make_async_copy(src, dst, load.at[i]) for i, (src, dst) in enumerate(sources)]
     for copy in loads:
         copy.start()
@@ -127,23 +135,38 @@
         started.append(made)
         return made
 
+    length = len_ref[...]
+    inverse_len = 1.0 / length.astype(F32)
+    valid = iota((SEQ, 1), 0) < length
+    loads[0].wait()
+    normed, rstd_x = layer_norm(hist_ref[0].astype(F32))
+    xnorm[...] = normed
+    xn[...] = normed.astype(BF16)
+    for at in range(0, 4 * D, 256):
+        if at % D == 0:
+            loads[1 + at // D].wait()
+        gate = dot_nt(xn[...], w1_ref[at : at + 256, :])
+        value, slant = silu_and_slope(gate)
+        act[:, at : at + 256] = value.astype(BF16)
+        slope[:, at : at + 256] = slant
+
     rows_i, cols_i = iota((SEQ, SEQ), 0), iota((SEQ, SEQ), 1)
     eye = rows_i == cols_i
-    loads[0].wait()
-    loads[1].wait()
+    for copy in loads[5:]:
+        copy.wait()
     ids_row = ids_ref[...].astype(F32)
     ids = jnp.sum(jnp.where(eye, ids_row, 0.0), axis=1, keepdims=True).astype(jnp.int32)
-    high = (cols_i == ids // 128).astype(BF16)
+    high = (cols_i == part_of(ids, 128)).astype(BF16)
     lane128 = iota((SEQ, 128), 1)
-    low = lane128 == lax.rem(ids, 128)
+    low = lane128 == rest_of(ids, 128)
     places = place_ref[...]
-    owners = dot_nn(high, (places // 256).astype(BF16))
+    owners = dot_nn(high, part_of(places, 256).astype(BF16))
     owner = jnp.sum(jnp.where(low, owners, 0.0), axis=1, keepdims=True).astype(jnp.int32)
-    locals_ = dot_nn(high, lax.rem(places, 256).astype(BF16))
+    locals_ = dot_nn(high, rest_of(places, 256).astype(BF16))
     local = jnp.sum(jnp.where(low, locals_, 0.0), axis=1, keepdims=True)
-    step_x = lax.rem(owner // 32 - x + NX, NX)
-    step_z = lax.rem(lax.rem(owner // 2, 16) - z + NZ, NZ)
-    step_c = lax.rem(lax.rem(owner, 2) - c + NC, NC)
+    step_x = rest_of(part_of(owner, 32) - x + NX, NX)
+    step_z = rest_of(part_of(owner, 2) - z + NZ, NZ)
+    step_c = rest_of(owner - c + NC, NC)
     order_x = jnp.where(step_x == 2, 3, jnp.where(step_x == 3, 2, step_x))
     block = ((order_x * NC + step_c) * NZ + step_z).astype(F32)
     block_row = jnp.sum(jnp.where(eye, block, 0.0), axis=0, keepdims=True)
@@ -158,21 +181,6 @@
         meta_s[lane] = found
         if lane == 0:
             meta_1[0, 0] = found
-
-    length = len_ref[...]
-    inverse_len = 1.0 / length.astype(F32)
-    valid = iota((SEQ, 1), 0) < length
-    loads[2].wait()
-    normed, rstd_x = layer_norm(hist_ref[0].astype(F32))
-    xnorm[...] = normed
-    xn[...] = normed.astype(BF16)
-    for at in range(0, 4 * D, 256):
-        if at % D == 0:
-            loads[3 + at // D].wait()
-        gate = dot_nt(xn[...], w1_ref[at : at + 256, :])
-        value, slant = silu_and_slope(gate)
-        act[:, at : at + 256] = value.astype(BF16)
-        slope[:, at : at + 256] = slant
 
     scale = 1.0 / 64**0.5
     mask = jnp.where((cols_i <= rows_i) & valid & (cols_i < length), inverse_len, 0.0)
@@ -199,7 +207,6 @@
         attn[:, at : at + 128] = total
 
     o_norm, rstd_o = layer_norm(attn[...])
-    loads[7].wait()
     dy = jnp.where(valid, dout_ref[0].astype(F32), 0.0)
     d_g[:, :D] = (dy * o_norm * slope[:, :D]).astype(BF16)
     d_on = dy * act[:, :D].astype(F32)
@@ -239,6 +246,9 @@
         for q in range(NY):
             out_s[lane, q] = moved[:, 128 * q : 128 * q + 128]
 
+    to_r, from_r = iota((SEQ, SEQ), 0), iota((SEQ, SEQ), 1)
+    order = (part_of(to_r, 16) == part_of(rest_of(from_r, 64), CAP)) & (part_of(rest_of(to_r, 16), CAP) == part_of(from_r, 64))
+    order = (order & (rest_of(to_r, CAP) == rest_of(from_r, CAP))).astype(BF16)
     pl.semaphore_wait(barrier, len(partners))
     meta_copies, lane_copies = {}, {}
 
@@ -255,9 +265,6 @@
     to_lanes(*range(8))
     lane_s[0, 0] = out_s[0, y]
 
-    to_r, from_r = iota((SEQ, SEQ), 0), iota((SEQ, SEQ), 1)
-    order = (to_r // 16 == lax.rem(from_r, 64) // CAP) & (lax.rem(to_r, 16) // CAP == from_r // 64)
-    order = (order & (lax.rem(to_r, CAP) == lax.rem(from_r, CAP))).astype(BF16)
     near_copies, relay_copies = [], ([], [])
 
     def pass_on(group):
@@ -303,12 +310,12 @@
     for lane in range(8):
         for copy in meta_copies[lane]:
             copy.wait_recv()
-    same_rank = lax.rem(iota((128, 128), 0), CAP) == lax.rem(iota((128, 128), 1), CAP)
+    same_rank = rest_of(iota((128, 128), 0), CAP) == rest_of(iota((128, 128), 1), CAP)
     tall = jnp.concatenate([meta_1[lane, d] for lane in range(8) for d in range(NY)], axis=0)
     tall = jnp.broadcast_to(tall[None], (NZ, 32, 128))
-    tall = jnp.where(iota((NZ, 32, 128), 2) // CAP == iota((NZ, 32, 128), 0), tall, 0.0)
+    tall = jnp.where(part_of(iota((NZ, 32, 128), 2), CAP) == iota((NZ, 32, 128), 0), tall, 0.0)
     lines = dot_nn(tall.reshape(512, 128).astype(BF16), same_rank.astype(BF16)).reshape(NZ, 32, 128)
-    lines = jnp.where(iota((NZ, 32, 128), 2) // CAP == iota((NZ, 32, 128), 1), lines, 0.0)
+    lines = jnp.where(part_of(iota((NZ, 32, 128), 2), CAP) == iota((NZ, 32, 128), 1), lines, 0.0)
     lines = jnp.sum(lines, axis=1)
     for d in range(NZ):
         meta_z[d] = lines[d : d + 1]
@@ -393,12 +400,6 @@
         )
         zt_copies.append(remote(zt_s.at[lax.rem(z + d % NZ, NZ)], zt_near.at[at], place(0, 0, d, 0)))
 
-    for copy in sum_copies:
-        copy.wait_recv()
-    tg_s[...] = (table + (sum_r[0].astype(F32) + sum_r[1].astype(F32))).astype(BF16)
-    tg_copies = {d: remote(tg_s, tg_r.at[d - 1], place(d, 0, 0, 0)) for d in STEPS_4}
-    table_ref[:, pl.ds(pl.multiple_of(y * 128, 128), 128)] = tg_s[...].astype(F32)
-
     for copy in zt_copies:
         copy.wait_recv()
     zt_sum_copies = []
@@ -411,6 +412,12 @@
     tile = zt_own[z]
     for i in range(6):
         tile += zt_near[i].astype(F32)
+
+    for copy in sum_copies:
+        copy.wait_recv()
+    tg_s[...] = (table + (sum_r[0].astype(F32) + sum_r[1].astype(F32))).astype(BF16)
+    tg_copies = {d: remote(tg_s, tg_r.at[d - 1], place(d, 0, 0, 0)) for d in STEPS_4}
+    table_ref[:, pl.ds(pl.multiple_of(y * 128, 128), 128)] = tg_s[...].astype(F32)
 
     for d, copy in tg_copies.items():
         copy.wait_recv()

time: 64.5 us -> 64 us (level)
  no operation moved by 1% of the time
where the time goes in v3:
time: 64 us; the launch traced here: 63.8 us
  Pallas kernels  59.3 us (93%)
  local copies, waits for them, and re-layouts  3.16 us (5%)
  between operations  1.28 us (2%)
    pallas_call x1, Pallas kernels, body(): pl.pallas_call(kernel, out_shape=(jax.ShapeDtypeStruct((SEQ, D), F32), ja...  59.3 us
    unnamed x2, local copies, waits for them, and re-layouts  3.16 us

profile of v3, /device:TPU:1, one launch (start us, length us, event | category | flops | bytes accessed | tf_op | source)
XLA Modules:
  0.0 63.8 jit_solution(13237097130753853255)
XLA Ops:
  1.3 59.3 %shard_map.77 = (f32[256,512]{1,0:T(8,128)}, f32[4,512]{1,0:T(4,128)}) custom-call(bf16[1,256,512]{2,1,0:T(8,128)(2,1)} %hist_any.1, bf16[1,256,512]{2,1,0:T(8,128)(2,1)} %dout_any.1, s32[1,1]{1,0:T(1,128)} %bitcast.2.len_ref, s32[1,256]{1,0:T(1,128)} %ids_any.1, s32[256,128]{1,0:T(8,128)} %bitcast.3, bf16[2048,512]{1,0:T(8,128)(2,1)} %w1_any.1), custom_call_target="tpu_custom_call" | custom-call | flops 4000000000 | bytes 8000000 | tf_op jit(solution)/shard_map/pallas_call | solution.py:506
  60.6 1.9 %copy.11 = f32[256,512]{1,0:T(8,128)} copy(f32[256,512]{1,0:T(8,128)} %get-tuple-element.4) | data formatting | bytes 1048576
  62.5 1.3 %copy.12 = f32[4,512]{1,0:T(4,128)} copy(f32[4,512]{1,0:T(4,128)} %get-tuple-element.5) | data formatting | bytes 16384

commit v4 on v3

--- a/solution.py
+++ b/solution.py
@@ -417,12 +417,12 @@
         copy.wait_recv()
     tg_s[...] = (table + (sum_r[0].astype(F32) + sum_r[1].astype(F32))).astype(BF16)
     tg_copies = {d: remote(tg_s, tg_r.at[d - 1], place(d, 0, 0, 0)) for d in STEPS_4}
-    table_ref[:, pl.ds(pl.multiple_of(y * 128, 128), 128)] = tg_s[...].astype(F32)
+    table_ref[:, pl.ds(pl.multiple_of(y * 128, 128), 128)] = tg_s[...]
 
     for d, copy in tg_copies.items():
         copy.wait_recv()
         source = lax.rem(y + NY - d, NY)
-        table_ref[:, pl.ds(pl.multiple_of(source * 128, 128), 128)] = tg_r[d - 1].astype(F32)
+        table_ref[:, pl.ds(pl.multiple_of(source * 128, 128), 128)] = tg_r[d - 1]
 
     for way, copy in enumerate(zt_sum_copies):
         copy.wait_recv()
@@ -503,10 +503,10 @@
     ]
     vmem = pl.BlockSpec(memory_space=pltpu.VMEM)
     hbm = pl.BlockSpec(memory_space=pltpu.HBM)
-    return pl.pallas_call(
+    table, weight = pl.pallas_call(
         kernel,
         out_shape=(
-            jax.ShapeDtypeStruct((SEQ, D), F32),
+            jax.ShapeDtypeStruct((SEQ, D), BF16),
             jax.ShapeDtypeStruct((4, D), F32),
         ),
         in_specs=[hbm, hbm, vmem, hbm, hbm, hbm],
@@ -517,6 +517,7 @@
         ),
         cost_estimate=pl.CostEstimate(flops=4 * 10**9, bytes_accessed=8 * 10**6, transcendentals=10**6),
     )(history, dout, lengths.reshape(1, 1), item_ids, row_place.reshape(256, 128), w1)
+    return table.astype(F32), weight
 
 
 def solution(mesh):

time: 64 us -> 63.8 us (level)
  local copies, waits for them, and re-layouts: 3.16 us -> 1.29 us
  other arithmetic: 0 us -> 1.8 us
    unnamed x2 -> x1, local copies, waits for them, and re-layouts: 3.16 us -> 1.29 us
    convert_element_type x0 -> x1, other arithmetic: none -> 1.8 us  [body(): return (table.astype(F32), weight)]
where the time goes in v4:
time: 63.8 us; the launch traced here: 63.6 us
  Pallas kernels  59.2 us (93%)
  other arithmetic  1.8 us (3%)
  local copies, waits for them, and re-layouts  1.29 us (2%)
  between operations  1.28 us (2%)
    pallas_call x1, Pallas kernels, body(): pl.pallas_call(kernel, out_shape=(jax.ShapeDtypeStruct((SEQ, D), BF16), j...  59.2 us
    convert_element_type x1, other arithmetic, body(): return (table.astype(F32), weight)  1.8 us
    unnamed x1, local copies, waits for them, and re-layouts  1.29 us

profile of v4, /device:TPU:1, one launch (start us, length us, event | category | flops | bytes accessed | tf_op | source)
XLA Modules:
  0.0 63.6 jit_solution(1889602886337810041)
XLA Ops:
  1.3 59.2 %shard_map.77 = (bf16[256,512]{1,0:T(8,128)(2,1)}, f32[4,512]{1,0:T(4,128)}) custom-call(bf16[1,256,512]{2,1,0:T(8,128)(2,1)} %hist_any.1, bf16[1,256,512]{2,1,0:T(8,128)(2,1)} %dout_any.1, s32[1,1]{1,0:T(1,128)} %bitcast.2.len_ref, s32[1,256]{1,0:T(1,128)} %ids_any.1, s32[256,128]{1,0:T(8,128)} %bitcast.3, bf16[2048,512]{1,0:T(8,128)(2,1)} %w1_any.1), custom_call_target="tpu_custom_call" | custom-call | flops 4000000000 | bytes 8000000 | tf_op jit(solution)/shard_map/pallas_call | solution.py:506
  60.5 1.8 %convert_element_type.3 = f32[256,512]{1,0:T(8,128)} convert(bf16[256,512]{1,0:T(8,128)(2,1)} %get-tuple-element.4) | non-fusion elementwise | flops 131072 | bytes 786432 | tf_op jit(solution)/shard_map/convert_element_type | solution.py:520
  62.3 1.3 %copy.10 = f32[4,512]{1,0:T(4,128)} copy(f32[4,512]{1,0:T(4,128)} %get-tuple-element.9) | data formatting | bytes 16384
